TPU v7x, 128 devices: a whole 4x4x4 slice. The times are simulated.
128 devices in a mesh: row: 8 (over z, x_lo), col: 16 (over x_hi, y, core).
Axes of the slice: x: 4 (x_hi: 2, x_lo: 2; x = x_hi * 2 + x_lo), y: 4, z: 4, core: 2. Of those that a mesh axis runs over, the one named last changes fastest.
Arguments:
- points_gen: bfloat16 [24576, 128], P(('row', 'col')), may hold values from -6 to 6
- points_obs: bfloat16 [16384, 128], P(('col', 'row')), may hold values from -6 to 6
- log_mass_gen: float32 [24576], P('row'), may hold values from -1 to 1
- log_mass_obs: float32 [16384], P('col'), may hold values from -1 to 1
Outputs:
- potential_gen: float32 [24576], P('row')
- potential_obs: float32 [16384], P('col')
- costate: float32 [24576, 128], P(('row', 'col'))
All inputs are finite; a program needn't handle non-finite values.
Results may differ from a plain program's by a relative error of at most 0.0015.
Values may be sent and summed in bfloat16 or wider, within the bound.
No kernel may reach another device: no remote copies, remote signals or barrier semaphores. Data moves between devices by JAX's collectives and lax.ppermute only.
A program may use at most 64 MiB of HBM per device.

v0:
```python
import functools
import math

import jax
import jax.numpy as jnp
from jax import lax
from jax.experimental import pallas as pl
from jax.experimental.pallas import tpu as pltpu
from jax.sharding import PartitionSpec as P

ITERS = 4
LANES = 128
CHUNK = 256
SAMPLE = 128
LOW, HIGH = 1e-20, 1e30
STEEP, FAINT, NOTHING = 20.0, 60.0, 60.0
VMEM = pl.BlockSpec(memory_space=pltpu.VMEM)
SMEM = pl.BlockSpec(memory_space=pltpu.SMEM)
NT = (((1,), (1,)), ((), ()))


def lse_over(parts):
    top = functools.reduce(jnp.maximum, parts)
    return top + jnp.log(sum(jnp.exp(part - top) for part in parts))


def planes(ref):
    return [ref[k] for k in range(ref.shape[0])]


def scores(left, right, left_wide):
    prod = lax.dot_general(left, right, NT, preferred_element_type=jnp.float32)
    return prod + jnp.concatenate([left_wide] * (right.shape[0] // LANES), axis=1)


def fold(values, op):
    rows, width = values.shape
    return op(values.reshape(rows // 8, 8, width), axis=0)


def store_row(ref, first, row):
    for part in range(row.shape[1] // LANES):
        ref[pl.ds(first + part, 1), :] = row[:, part * LANES : (part + 1) * LANES]


def dense_of(row):
    return jnp.concatenate([row[:, k * LANES : (k + 1) * LANES] for k in range(row.shape[1] // LANES)], axis=0)


def row_of(dense):
    return jnp.concatenate([dense[k : k + 1, :] for k in range(dense.shape[0])], axis=1)


def widen(dense, wide_ref):
    for part in range(dense.shape[0]):
        row = jnp.broadcast_to(dense[part : part + 1, :], (LANES, LANES))
        wide_ref[part * LANES : (part + 1) * LANES, :] = jnp.transpose(row)


def squares(points):
    wide = points.astype(jnp.float32)
    square = wide * wide
    high = square.astype(jnp.bfloat16)
    low = (square - high.astype(jnp.float32)).astype(jnp.bfloat16)
    ones = jnp.ones((8, LANES), jnp.bfloat16)
    row = lax.dot_general(ones, high, NT, preferred_element_type=jnp.float32)
    row += lax.dot_general(ones, low, NT, preferred_element_type=jnp.float32)
    return dense_of(row[:1, :])


def in_parts(row):
    high = row.astype(jnp.bfloat16).astype(jnp.float32)
    middle = (row - high).astype(jnp.bfloat16).astype(jnp.float32)
    low = row - high - middle
    line = lax.broadcasted_iota(jnp.int32, (16, row.shape[1]), 0)
    parts = jnp.where(line == 0, high, jnp.where(line == 1, middle, jnp.where(line == 2, low, 0.0)))
    return parts.astype(jnp.bfloat16)


def means_of(left_ref, chunk, values, mean_ref):
    left_t = jnp.transpose(left_ref[...].astype(jnp.float32))
    left_t = jnp.concatenate([left_t, jnp.ones((16, left_t.shape[1]), jnp.float32)], axis=0).astype(jnp.bfloat16)
    numer = jnp.dot(left_t, values.astype(jnp.bfloat16), preferred_element_type=jnp.float32)
    mean = numer[:LANES, :] / numer[LANES : LANES + 1, :]
    mean_ref[pl.ds(pl.multiple_of(chunk * CHUNK, CHUNK), CHUNK), :] = jnp.transpose(mean)


def exact_pass(left_ref, right_ref, wide_ref, shift_ref, total_ref, mean_ref=None):
    n, m = left_ref.shape[0], right_ref.shape[0]
    block = 512
    per = CHUNK // LANES

    def one(chunk, carry):
        right = right_ref[pl.ds(pl.multiple_of(chunk * CHUNK, CHUNK), CHUNK), :]

        def largest(step, top):
            rows = pl.ds(pl.multiple_of(step * block, block), block)
            return jnp.maximum(top, fold(scores(left_ref[rows, :], right, wide_ref[rows, :]), jnp.max))

        top = lax.fori_loop(0, n // block, largest, jnp.full((8, CHUNK), -3e38, jnp.float32))
        top = jnp.max(top, axis=0, keepdims=True)

        def add(step, total):
            rows = pl.ds(pl.multiple_of(step * block, block), block)
            return total + fold(jnp.exp(scores(left_ref[rows, :], right, wide_ref[rows, :]) - top), jnp.sum)

        total = lax.fori_loop(0, n // block, add, jnp.zeros((8, CHUNK), jnp.float32))
        store_row(shift_ref, chunk * per, top)
        store_row(total_ref, chunk * per, jnp.sum(total, axis=0, keepdims=True))
        if mean_ref is not None:
            means_of(left_ref, chunk, jnp.exp(scores(left_ref[...], right, wide_ref[...]) - top), mean_ref)
        return carry

    lax.fori_loop(0, m // CHUNK, one, 0)


def sampled_pass(left_ref, right_ref, wide_ref, shift_ref, total_ref, matrix_ref=None):
    m = right_ref.shape[0]
    per = CHUNK // LANES
    for chunk in range(m // CHUNK):
        right = right_ref[chunk * CHUNK : (chunk + 1) * CHUNK, :]
        some = scores(left_ref[:SAMPLE, :], right, wide_ref[:SAMPLE, :])
        shift = jnp.max(fold(some, jnp.max), axis=0, keepdims=True)
        values = jnp.exp(scores(left_ref[...], right, wide_ref[...]) - shift)
        total = jnp.sum(fold(values, jnp.sum), axis=0, keepdims=True)
        store_row(shift_ref, chunk * per, shift)
        store_row(total_ref, chunk * per, total)
        if matrix_ref is not None:
            matrix_ref[:, chunk * CHUNK : (chunk + 1) * CHUNK] = values.astype(jnp.bfloat16)

    @pl.when(jnp.logical_not(jnp.max(total_ref[...]) < HIGH))
    def _():
        exact_pass(left_ref, right_ref, wide_ref, shift_ref, total_ref)
        if matrix_ref is not None:
            for chunk in range(m // CHUNK):
                across = pl.ds(chunk * CHUNK, CHUNK)
                top = row_of(shift_ref[chunk * per : (chunk + 1) * per, :])
                values = jnp.exp(scores(left_ref[...], right_ref[across, :], wide_ref[...]) - top)
                matrix_ref[:, across] = values.astype(jnp.bfloat16)

    return shift_ref[...] + jnp.log(total_ref[...])


def spread(out_ref, value):
    for copy in range(out_ref.shape[0]):
        out_ref[copy] = value


def of_core(dense, core, count):
    swapped = pltpu.roll(dense, LANES // 2, axis=1)
    left = lax.broadcasted_iota(jnp.int32, (1, LANES), 1) < LANES // 2
    halves = dense.shape[0] // count
    chosen = []
    for parity in range(2):
        sources = [(2 * k + parity) * halves + t for k in range(count) for t in range(halves)]
        rows = []
        for one, two in zip(sources[::2], sources[1::2]):
            first = (swapped if one % 2 else dense)[one // 2 : one // 2 + 1, :]
            second = (dense if two % 2 else swapped)[two // 2 : two // 2 + 1, :]
            rows.append(jnp.where(left, first, second))
        chosen.append(jnp.concatenate(rows, axis=0))
    return jnp.where(core == 0, chosen[0], chosen[1])


def half_kernel(count, core_ref, same_ref, right_ref, mass_ref, out_ref, right_sq_ref, wide_ref, shift_ref, total_ref):
    right_sq_ref[...] = squares(right_ref[...])
    mass = of_core(mass_ref[...], core_ref[0], count)
    widen(mass - 0.5 * squares(same_ref[...]), wide_ref)
    out_ref[...] = sampled_pass(same_ref, right_ref, wide_ref, shift_ref, total_ref)


def first_kernel(
    count, core_ref, same_ref, other_ref, right_ref, mass_ref, half_ref,
    out_ref, left_ref, sq_ref, wide_ref, shift_ref, total_ref,
):
    core = core_ref[0]
    own = same_ref.shape[0] // count
    for k in range(count):
        rows = pl.ds(k * own, own)
        left_ref[pl.ds(pl.multiple_of((2 * k + core) * own, 64), own), :] = same_ref[rows, :]
        left_ref[pl.ds(pl.multiple_of((2 * k + 1 - core) * own, 64), own), :] = other_ref[rows, :]
    sq_ref[...] = squares(left_ref[...])
    mass = of_core(mass_ref[...], 1 - core, count)
    widen(mass - 0.5 * squares(other_ref[...]), wide_ref)
    result = sampled_pass(other_ref, right_ref, wide_ref, shift_ref, total_ref)
    spread(out_ref, lse_over([half_ref[...], result]))


def second_kernel(
    left_ref, right_ref, mass_ref, from_ref,
    out_ref, left_add_ref, right_add_ref, matrix_ref, wide_ref, shift_ref, total_ref,
):
    offset = 2.0 * mass_ref[...] - lse_over(planes(from_ref))
    left_add_ref[...] = offset
    widen(offset, wide_ref)
    spread(out_ref, sampled_pass(left_ref, right_ref, wide_ref, shift_ref, total_ref, matrix_ref))
    right_add_ref[...] = -shift_ref[...]


def close_pass(left_ref, right_ref, offset, bad, add_ref, wide_ref, shift_ref, total_ref, mean_ref=None):
    shift_ref[...] = -add_ref[...]
    totals = total_ref[...]
    fits = (totals > LOW) & (totals < HIGH)
    marks = [jnp.where(mask, 1.0, 0.0) for mask in (bad, jnp.logical_not(fits))]
    flags = [mark[k : k + 8, :] for mark in marks for k in range(0, mark.shape[0], 8)]

    @pl.when(jnp.max(functools.reduce(jnp.maximum, flags)) > 0.0)
    def _():
        widen(offset, wide_ref)
        exact_pass(left_ref, right_ref, wide_ref, shift_ref, total_ref, mean_ref)


def col_kernel(
    matrix_ref, obs_ref, gen_ref, mass_ref, from_ref, first_ref, obs_add_ref, gen_add_ref,
    out_ref, wide_ref, shift_ref, total_ref,
):
    offset = 2.0 * mass_ref[...] - lse_over(planes(from_ref))
    gain = offset - gen_add_ref[...]
    level = offset + first_ref[0]
    factors = jnp.exp(gain)
    for block in range(obs_ref.shape[0] // LANES):
        rows = pl.ds(block * LANES, LANES)
        total = jnp.zeros((LANES, LANES), jnp.float32)
        for part in range(gain.shape[0]):
            values = matrix_ref[rows, part * LANES : (part + 1) * LANES].astype(jnp.float32)
            total += values * factors[part : part + 1, :]
        total_ref[block : block + 1, :] = jnp.sum(jnp.transpose(total), axis=0, keepdims=True)
    bad = (level > STEEP) | ((gain < -FAINT) & (level > -NOTHING))
    close_pass(gen_ref, obs_ref, offset, bad, obs_add_ref, wide_ref, shift_ref, total_ref)
    spread(out_ref, shift_ref[...] + jnp.log(total_ref[...]))


def row_kernel(
    matrix_ref, obs_ref, gen_ref, mass_ref, from_ref, obs_add_ref, gen_add_ref,
    out_ref, wide_ref, shift_ref, total_ref,
):
    offset = 2.0 * mass_ref[...] - lse_over(planes(from_ref))
    gain = offset - obs_add_ref[...]
    total = jnp.dot(in_parts(row_of(jnp.exp(gain))), matrix_ref[...], preferred_element_type=jnp.float32)
    total_ref[...] = dense_of(jnp.sum(total[:8, :], axis=0, keepdims=True))
    close_pass(obs_ref, gen_ref, offset, wild(gain), gen_add_ref, wide_ref, shift_ref, total_ref)
    spread(out_ref, shift_ref[...] + jnp.log(total_ref[...]))


def wild(gain):
    return (gain > STEEP) | (gain < -FAINT)


def mean_kernel(
    core_ref, matrix_ref, left_ref, right_ref, mass_ref, from_ref, left_add_ref, right_add_ref, left_sq_ref,
    potential_ref, out_ref, keep_ref, send_ref, wide_ref, shift_ref, total_ref, mean_ref,
):
    offset = 2.0 * mass_ref[...] - lse_over(planes(from_ref))
    potential_ref[...] = 2.0 * (offset - mass_ref[...]) + left_sq_ref[...]
    gain = offset - left_add_ref[...]
    weight = row_of(jnp.exp(gain))
    left_t = jnp.transpose(left_ref[...].astype(jnp.float32)) * weight
    high = left_t.astype(jnp.bfloat16)
    low = (left_t - high.astype(jnp.float32)).astype(jnp.bfloat16)
    factors = jnp.concatenate([high, low, in_parts(weight)], axis=0)
    for chunk in range(right_ref.shape[0] // CHUNK):
        across = pl.ds(chunk * CHUNK, CHUNK)
        sums = jnp.dot(factors, matrix_ref[:, across], preferred_element_type=jnp.float32)
        total = jnp.sum(sums[2 * LANES : 2 * LANES + 8, :], axis=0, keepdims=True)
        store_row(total_ref, chunk * CHUNK // LANES, total)
        mean_ref[across, :] = jnp.transpose((sums[:LANES, :] + sums[LANES : 2 * LANES, :]) / total)
    close_pass(left_ref, right_ref, offset, wild(gain), right_add_ref, wide_ref, shift_ref, total_ref, mean_ref)
    out_ref[...] = shift_ref[...] + jnp.log(total_ref[...])
    core = core_ref[0]
    count, own, _ = keep_ref.shape
    for k in range(count):
        keep_ref[k] = mean_ref[pl.ds(pl.multiple_of((2 * k + core) * own, 64), own), :]
        send_ref[k] = mean_ref[pl.ds(pl.multiple_of((2 * k + 1 - core) * own, 64), own), :]


def pair_kernel(core_ref, keep_ref, came_ref, lse_ref, came_lse_ref, out_ref, wide_ref):
    core = core_ref[0]
    count, own, _ = keep_ref.shape
    both = lse_over([lse_ref[...], came_lse_ref[...]])
    lines = both.shape[0]
    spaced = both * 8193.0
    high = spaced - (spaced - both)
    low = both - high
    widen(jnp.exp(lse_ref[...] - both), wide_ref)
    for k in range(count):
        share = wide_ref[pl.ds(pl.multiple_of((2 * k + core) * own, 64), own), :]
        out_ref[k, :own, :] = came_ref[k] + share * (keep_ref[k] - came_ref[k])
        out_ref[k, own : own + lines, :] = high
        out_ref[k, own + lines :, :] = low


def last_kernel(col_ref, all_ref, points_ref, mass_ref, sq_ref, gen_ref, costate_ref, share_ref, wide_ref):
    own = points_ref.shape[0]
    count = all_ref.shape[0]
    lines = mass_ref.shape[0]
    parts = [all_ref[k, own : own + lines, :] + all_ref[k, own + lines :, :] for k in range(count)]
    total = lse_over(parts)
    gen_ref[...] = 2.0 * mass_ref[...] + sq_ref[...] - 2.0 * total
    first = col_ref[0] * own
    line = first // LANES
    inside = pl.multiple_of(first - line * LANES, 64)
    result = points_ref[...].astype(jnp.float32)
    span = wide_ref.shape[1] // LANES
    for k in range(count):
        share_ref[k] = jnp.exp(parts[k] - total)
        for part in range(span):
            row = jnp.broadcast_to(share_ref[k, pl.ds(line + part, 1), :], (LANES, LANES))
            wide_ref[k, part * LANES : (part + 1) * LANES, :] = jnp.transpose(row)
        result -= wide_ref[k, pl.ds(inside, own), :] * all_ref[k, :own, :]
    costate_ref[...] = result


def call(kernel, ins, outs, scratch, flops=0, exps=0, room=28):
    moved = sum(math.prod(x.shape) * x.dtype.itemsize for x in list(ins) + list(outs))
    return pl.pallas_call(
        kernel,
        out_shape=outs,
        in_specs=[SMEM if x.dtype == jnp.int32 else VMEM for x in ins],
        out_specs=[VMEM] * len(outs),
        scratch_shapes=scratch,
        compiler_params=pltpu.CompilerParams(vmem_limit_bytes=room * 2**20),
        cost_estimate=pl.CostEstimate(flops=flops, bytes_accessed=moved, transcendentals=exps),
    )(*ins)


def f32(*shape):
    return jax.ShapeDtypeStruct(shape, jnp.float32)


def wide_scratch(n):
    return pltpu.VMEM((n, LANES), jnp.float32)


def body(n_row, n_col, points_gen, points_obs, log_mass_gen, log_mass_obs):
    own = points_gen.shape[0]
    half = n_col // 2
    groups = [list(range(core, n_col, 2)) for core in range(2)]
    pair = [(k, k ^ 1) for k in range(n_col)]
    col = lax.axis_index("col").astype(jnp.int32)
    core = lax.rem(col, 2).reshape(1)
    n, m = own * n_col, points_obs.shape[0] * n_row
    lines, obs_lines = n // LANES, m // LANES

    def over_row(blocks):
        return lax.all_to_all(blocks, "row", 0, 0)

    def over_col(blocks):
        return lax.all_to_all(blocks, "col", 0, 0)

    def over_chips(blocks):
        return lax.all_to_all(blocks, "col", 0, 0, axis_index_groups=groups)

    mass_gen = log_mass_gen.reshape(lines, LANES)
    mass_obs = log_mass_obs.reshape(obs_lines, LANES)
    same = over_chips(jnp.broadcast_to(points_gen[None], (half,) + points_gen.shape))
    obs_copies = jnp.broadcast_to(points_obs[None], (n_row,) + points_obs.shape)
    same, obs_copies = lax.optimization_barrier((same, obs_copies))
    obs, same = lax.optimization_barrier((over_row(obs_copies).reshape(m, LANES), same))
    other = lax.ppermute(same, "col", pair)

    cost = dict(flops=2 * n * m * LANES, exps=n * m)
    product_cost = dict(flops=2 * n * m * LANES)
    small, gen_small = wide_scratch(obs_lines), wide_scratch(lines)
    col_out, row_out = f32(n_row, obs_lines, LANES), f32(n_col, lines, LANES)
    same, other = same.reshape(n // 2, LANES), other.reshape(n // 2, LANES)
    half_cost = dict(flops=n * m * LANES, exps=n * m // 2)
    half_own, obs_sq = call(
        functools.partial(half_kernel, half),
        (core, same, obs, mass_gen),
        [f32(obs_lines, LANES), f32(obs_lines, LANES)],
        [wide_scratch(n // 2), small, small],
        **half_cost,
    )
    col_own, gen, gen_sq = call(
        functools.partial(first_kernel, half),
        (core, same, other, obs, mass_gen, half_own),
        [col_out, jax.ShapeDtypeStruct((n, LANES), points_gen.dtype), f32(lines, LANES)],
        [wide_scratch(n // 2), small, small],
        **half_cost,
    )
    col_all = over_row(col_own)
    row_own, obs_add, gen_add, matrix = call(
        second_kernel,
        (obs, gen, mass_obs, col_all),
        [row_out, f32(obs_lines, LANES), f32(lines, LANES), jax.ShapeDtypeStruct((m, n), jnp.bfloat16)],
        [wide_scratch(m), gen_small, gen_small],
        **cost,
    )
    row_all = over_col(row_own)
    first = row_own
    for step in range(1, ITERS):
        (col_own,) = call(
            col_kernel,
            (matrix, obs, gen, mass_gen, row_all, first, obs_add, gen_add),
            [col_out],
            [wide_scratch(n), small, small],
            **product_cost,
        )
        col_all = over_row(col_own)
        if step == ITERS - 1:
            break
        (row_own,) = call(
            row_kernel,
            (matrix, obs, gen, mass_obs, col_all, obs_add, gen_add),
            [row_out],
            [wide_scratch(m), gen_small, gen_small],
            **product_cost,
        )
        row_all = over_col(row_own)
    potential_obs, row_lse, keep, send = call(
        mean_kernel,
        (core, matrix, obs, gen, mass_obs, col_all, obs_add, gen_add, obs_sq),
        [f32(obs_lines, LANES), f32(lines, LANES), f32(half, own, LANES), f32(half, own, LANES)],
        [wide_scratch(m), gen_small, gen_small, wide_scratch(n)],
        **product_cost,
    )
    came = lax.ppermute(send.astype(jnp.float16), "col", pair).astype(jnp.float32)
    came_lse = lax.ppermute(row_lse, "col", pair)
    (joined,) = call(
        pair_kernel, (core, keep, came, row_lse, came_lse), [f32(half, own + 2 * lines, LANES)], [wide_scratch(n)]
    )
    joined_all = over_chips(joined.astype(jnp.float16)).astype(jnp.float32)
    span = own // LANES + 1
    potential_gen, costate = call(
        last_kernel,
        (col.reshape(1), joined_all, points_gen, mass_gen, gen_sq),
        [f32(lines, LANES), f32(own, LANES)],
        [pltpu.VMEM((half, lines, LANES), jnp.float32), pltpu.VMEM((half, span * LANES, LANES), jnp.float32)],
    )
    return potential_gen.reshape(-1), potential_obs.reshape(-1), costate


def solution(mesh):
    return jax.shard_map(
        functools.partial(body, mesh.shape["row"], mesh.shape["col"]),
        mesh=mesh,
        in_specs=(P(("row", "col"), None), P(("col", "row"), None), P("row"), P("col")),
        out_specs=(P("row"), P("col"), P(("row", "col"), None)),
        check_vma=False,
    )
```

profile of v0, /device:TPU:0, one launch (start us, length us, event | category | flops | bytes accessed | tf_op | source)
XLA Modules:
  0.0 194.3 jit_solution(13378134897765030759)
XLA Ops:
  0.6 0.9 broadcast_in_dim.4
  1.5 17.0 %all_to_all.50 = bf16[8,192,128]{2,1,0:T(8,128)(2,1)S(1)} all-to-all(bf16[8,192,128]{2,1,0:T(8,128)(2,1)S(1)} %broadcast_in_dim.4), channel_id=1, replica_groups={{0,2,4,6,8,10,12,14},{1,3,5,7,9,11,13,15},{16,18,20,22,24,26,28,30},{17..., dimensions={0} | all-to-all | bytes 786432 | tf_op jit(solution)/shard_map/all_to_all | solution.py:351
  18.5 0.8 broadcast_in_dim.5
  19.3 12.4 %all_to_all.51 = bf16[8,128,128]{2,1,0:T(8,128)(2,1)S(1)} all-to-all(bf16[8,128,128]{2,1,0:T(8,128)(2,1)S(1)} %broadcast_in_dim.5), channel_id=1, replica_groups=mesh['row'=8,'col'=16] {'row'}, dimensions={0} | all-to-all | bytes 524288 | tf_op jit(solution)/shard_map/all_to_all | solution.py:345
  31.7 0.0 collective-permute-start
  31.7 0.8 copy-done
  32.5 1.8 shard_map.67
  34.3 2.2 %shard_map.68 = (f32[8,8,128]{2,1,0:T(8,128)S(1)}, bf16[3072,128]{1,0:T(8,128)(2,1)S(1)}, f32[24,128]{1,0:T(8,128)S(1)}) custom-call(s32[1]{0:T(128)} %bitcast.1.core_ref, bf16[1536,128]{1,0:T(8,128)(2,1)S(1)} %bitcast.19, bf16[1536,128]{1,0:T(8,128)(2,1)S(1)} %bitcast.30, bf16[1024,128]{1,0:T(8,128)(2,1)S(1)} %bitcast.10, f32[24,128]{1,0:T(8,128)S(1)} %bitcast.21, ...), custom_call_target="tpu_custom_call" | custom-call | flops 402653184 | bytes 1896452 | tf_op jit(solution)/shard_map/pallas_call | solution.py:315
  36.5 8.8 %all_to_all.52.from_ref = f32[8,8,128]{2,1,0:T(8,128)S(1)} all-to-all(f32[8,8,128]{2,1,0:T(8,128)S(1)} %get-tuple-element.28), channel_id=1, replica_groups=mesh['row'=8,'col'=16] {'row'}, dimensions={0} | all-to-all | bytes 65536 | tf_op jit(solution)/shard_map/all_to_all | solution.py:345
  45.3 17.4 %shard_map.69 = (f32[16,24,128]{2,1,0:T(8,128)S(1)}, f32[8,128]{1,0:T(8,128)S(1)}, f32[24,128]{1,0:T(8,128)S(1)}, bf16[1024,3072]{1,0:T(8,128)(2,1)S(1)}) custom-call(bf16[1024,128]{1,0:T(8,128)(2,1)S(1)} %bitcast.11, bf16[3072,128]{1,0:T(8,128)(2,1)S(1)} %get-tuple-element.27.right_ref.gen_ref, f32[8,128]{1,0:T(8,128)S(1)} %bitcast.26, ...), custom_call_target="tpu_custom_call" | custom-call | flops 805306368 | bytes 7589888 | tf_op jit(solution)/shard_map/pallas_call | solution.py:315
  62.7 16.6 %all_to_all.53.from_ref = f32[16,24,128]{2,1,0:T(8,128)S(1)} all-to-all(f32[16,24,128]{2,1,0:T(8,128)S(1)} %get-tuple-element.30.first_ref), channel_id=1, replica_groups=mesh['row'=8,'col'=16] {'col'}, dimensions={0} | all-to-all | bytes 393216 | tf_op jit(solution)/shard_map/all_to_all | solution.py:348
  79.3 1.7 shard_map.70
  81.0 21.4 %all_to_all.54.from_ref = f32[8,8,128]{2,1,0:T(8,128)S(1)} all-to-all(f32[8,8,128]{2,1,0:T(8,128)S(1)} %shard_map.70), channel_id=1, replica_groups=mesh['row'=8,'col'=16] {'row'}, dimensions={0} | all-to-all | bytes 65536 | tf_op jit(solution)/shard_map/all_to_all | solution.py:345
  102.4 1.1 shard_map.71
  103.5 11.6 %all_to_all.55.from_ref = f32[16,24,128]{2,1,0:T(8,128)S(1)} all-to-all(f32[16,24,128]{2,1,0:T(8,128)S(1)} %shard_map.71), channel_id=1, replica_groups=mesh['row'=8,'col'=16] {'col'}, dimensions={0} | all-to-all | bytes 393216 | tf_op jit(solution)/shard_map/all_to_all | solution.py:348
  115.1 1.5 shard_map.72
  116.6 21.3 %all_to_all.56.from_ref = f32[8,8,128]{2,1,0:T(8,128)S(1)} all-to-all(f32[8,8,128]{2,1,0:T(8,128)S(1)} %shard_map.72), channel_id=1, replica_groups=mesh['row'=8,'col'=16] {'row'}, dimensions={0} | all-to-all | bytes 65536 | tf_op jit(solution)/shard_map/all_to_all | solution.py:345
  137.9 1.1 shard_map.73
  139.0 11.5 %all_to_all.57.from_ref = f32[16,24,128]{2,1,0:T(8,128)S(1)} all-to-all(f32[16,24,128]{2,1,0:T(8,128)S(1)} %shard_map.73), channel_id=1, replica_groups=mesh['row'=8,'col'=16] {'col'}, dimensions={0} | all-to-all | bytes 393216 | tf_op jit(solution)/shard_map/all_to_all | solution.py:348
  150.5 14.3 %shard_map.74 = f32[8,8,128]{2,1,0:T(8,128)S(1)} custom-call(bf16[1024,3072]{1,0:T(8,128)(2,1)S(1)} %get-tuple-element.29.matrix_ref, bf16[1024,128]{1,0:T(8,128)(2,1)S(1)} %bitcast.16, bf16[3072,128]{1,0:T(8,128)(2,1)S(1)} %get-tuple-element.27.right_ref.gen_ref, f32[24,128]{1,0:T(8,128)S(1)} %bitcast.24, f32[16,24,128]{2,1,0:T(8,128)S(1)} %all_to_all.57.from_ref, ...), custom_call_target="tpu_custom_call" | custom-call | flops 805306368 | bytes 7794688 | tf_op jit(solution)/shard_map/pallas_call | solution.py:315
  164.8 8.6 %all_to_all.58.from_ref = f32[8,8,128]{2,1,0:T(8,128)S(1)} all-to-all(f32[8,8,128]{2,1,0:T(8,128)S(1)} %shard_map.74), channel_id=1, replica_groups=mesh['row'=8,'col'=16] {'row'}, dimensions={0} | all-to-all | bytes 65536 | tf_op jit(solution)/shard_map/all_to_all | solution.py:345
  173.4 2.7 %shard_map.75 = (f32[8,128]{1,0:T(8,128)}, f32[24,128]{1,0:T(8,128)S(1)}, f32[8,192,128]{2,1,0:T(8,128)S(1)}, f32[8,192,128]{2,1,0:T(8,128)S(1)}) custom-call(s32[1]{0:T(128)} %bitcast.1.core_ref, bf16[1024,3072]{1,0:T(8,128)(2,1)S(1)} %get-tuple-element.29.matrix_ref, bf16[1024,128]{1,0:T(8,128)(2,1)S(1)} %bitcast.17, ...), custom_call_target="tpu_custom_call" | custom-call | flops 805306368 | bytes 8986628 | tf_op jit(solution)/shard_map/pallas_call | solution.py:315
  176.2 0.1 convert_element_type.12
  176.2 0.1 collective-permute-start.1
  176.3 0.5 collective-permute-start.2
  176.8 1.2 collective-permute-done.1
  178.1 0.1 convert_element_type.13.came_ref
  178.1 0.7 shard_map.76
  178.8 0.1 convert_element_type.14
  178.9 14.2 %all_to_all.59 = f16[8,240,128]{2,1,0:T(8,128)(2,1)S(1)} all-to-all(f16[8,240,128]{2,1,0:T(8,128)(2,1)S(1)} %convert_element_type.14), channel_id=1, replica_groups={{0,2,4,6,8,10,12,14},{1,3,5,7,9,11,13,15},{16,18,20,22,24,26,28,30},{17..., dimensions={0} | all-to-all | bytes 983040 | tf_op jit(solution)/shard_map/all_to_all | solution.py:351
  193.1 0.1 convert_element_type.15.all_ref
  193.2 1.1 shard_map.77
  (9 shorter events, 0.0 us)
Async XLA Ops:
  0.6 44.6 %copy-start.3 = (f32[1024]{0:T(1024)S(1)}, f32[1024]{0:T(1024)}, u32[]{:S(2)}) copy-start(f32[1024]{0:T(1024)} %param.7) | copy-start | bytes 12292
  31.7 47.6 %copy-start.1 = (f32[3072]{0:T(1024)S(1)}, f32[3072]{0:T(1024)}, u32[]{:S(2)}) copy-start(f32[3072]{0:T(1024)} %param.6) | copy-start | bytes 36868
  31.7 2.6 %collective-permute-start = (bf16[8,192,128]{2,1,0:T(8,128)(2,1)S(1)}, bf16[8,192,128]{2,1,0:T(8,128)(2,1)S(1)}, u32[]{:S(2)}, u32[]{:S(2)}) collective-permute-start(bf16[8,192,128]{2,1,0:T(8,128)(2,1)S(1)} %all_to_all.50), channel_id=1, source_target_pairs={{0,1},{1,0},{2,3},{3,2},{4,5},{5,4},{6,7},{7,6},{8,9},{9,8},{10,11... | collective-permute-start | bytes 1179656 | tf_op jit(solution)/shard_map/ppermute | solution.py:359
  31.7 0.8 copy-start
  173.4 19.7 %copy-start.2 = (bf16[192,128]{1,0:T(8,128)(2,1)S(1)}, bf16[192,128]{1,0:T(8,128)(2,1)}, u32[]{:S(2)}) copy-start(bf16[192,128]{1,0:T(8,128)(2,1)} %points_ref.1) | copy-start | bytes 147460
  176.2 1.8 collective-permute-start.1
  176.3 1.8 collective-permute-start.2
where the time goes:
time: 193 us; the launch traced here: 194 us
  blocking collectives  143 us (74%)
  Pallas kernels  45.7 us (24%)
  local copies, waits for them, and re-layouts  2.44 us (1%)
    all_to_all x5, blocking collectives, over_row(): return lax.all_to_all(blocks, 'row', 0, 0)  72.5 us
    pallas_call x11, Pallas kernels, call(): pl.pallas_call(kernel, out_shape=outs, in_specs=[SMEM if x.dtype == jnp.i...  45.7 us
    all_to_all x3, blocking collectives, over_col(): return lax.all_to_all(blocks, 'col', 0, 0)  39.6 us
    all_to_all x2, blocking collectives, over_chips(): return lax.all_to_all(blocks, 'col', 0, 0, axis_index_groups=groups)  31.2 us
  transfers between devices with their start and end apart: 3, of which 1 were waited for; matrix products, arithmetic and copies ran while one was open for 0% of the time, Pallas kernels for 1%

commit v1 on v0

--- a/solution.py
+++ b/solution.py
@@ -352,10 +352,10 @@
 
     mass_gen = log_mass_gen.reshape(lines, LANES)
     mass_obs = log_mass_obs.reshape(obs_lines, LANES)
-    same = over_chips(jnp.broadcast_to(points_gen[None], (half,) + points_gen.shape))
-    obs_copies = jnp.broadcast_to(points_obs[None], (n_row,) + points_obs.shape)
-    same, obs_copies = lax.optimization_barrier((same, obs_copies))
-    obs, same = lax.optimization_barrier((over_row(obs_copies).reshape(m, LANES), same))
+    obs = over_row(jnp.broadcast_to(points_obs[None], (n_row,) + points_obs.shape)).reshape(m, LANES)
+    gen_copies = jnp.broadcast_to(points_gen[None], (half,) + points_gen.shape)
+    obs, gen_copies = lax.optimization_barrier((obs, gen_copies))
+    same = over_chips(gen_copies)
     other = lax.ppermute(same, "col", pair)
 
     cost = dict(flops=2 * n * m * LANES, exps=n * m)

time: 193 us -> 189 us (0.979)
  blocking collectives: 143 us -> 138 us
    all_to_all x5, blocking collectives: 72.5 us -> 60.2 us  [over_row(): return lax.all_to_all(blocks, 'row', 0, 0)]
    all_to_all x3, blocking collectives: 39.6 us -> 47.4 us  [over_col(): return lax.all_to_all(blocks, 'col', 0, 0)]
where the time goes in v1:
time: 189 us
  blocking collectives  138 us (73%)
  Pallas kernels  45.6 us (24%)
  local copies, waits for them, and re-layouts  2.44 us (1%)
    all_to_all x5, blocking collectives, over_row(): return lax.all_to_all(blocks, 'row', 0, 0)  60.2 us
    all_to_all x3, blocking collectives, over_col(): return lax.all_to_all(blocks, 'col', 0, 0)  47.4 us
    pallas_call x11, Pallas kernels, call(): pl.pallas_call(kernel, out_shape=outs, in_specs=[SMEM if x.dtype == jnp.i...  45.6 us
    all_to_all x2, blocking collectives, over_chips(): return lax.all_to_all(blocks, 'col', 0, 0, axis_index_groups=groups)  30.1 us
  transfers between devices with their start and end apart: 3, of which 1 were waited for; matrix products, arithmetic and copies ran while one was open for 0% of the time, Pallas kernels for 1%

profile of v1, /device:TPU:0, one launch (start us, length us, event | category | flops | bytes accessed | tf_op | source)
XLA Modules:
  0.0 188.6 jit_solution(14216228660096644983)
XLA Ops:
  0.6 0.8 broadcast_in_dim.4
  1.4 13.4 %all_to_all.50 = bf16[8,128,128]{2,1,0:T(8,128)(2,1)S(1)} all-to-all(bf16[8,128,128]{2,1,0:T(8,128)(2,1)S(1)} %broadcast_in_dim.4), channel_id=1, replica_groups=mesh['row'=8,'col'=16] {'row'}, dimensions={0} | all-to-all | bytes 524288 | tf_op jit(solution)/shard_map/all_to_all | solution.py:345
  14.8 0.8 broadcast_in_dim.5
  15.7 15.9 %all_to_all.51 = bf16[8,192,128]{2,1,0:T(8,128)(2,1)S(1)} all-to-all(bf16[8,192,128]{2,1,0:T(8,128)(2,1)S(1)} %broadcast_in_dim.5), channel_id=1, replica_groups={{0,2,4,6,8,10,12,14},{1,3,5,7,9,11,13,15},{16,18,20,22,24,26,28,30},{17..., dimensions={0} | all-to-all | bytes 786432 | tf_op jit(solution)/shard_map/all_to_all | solution.py:351
  31.6 0.0 collective-permute-start
  31.6 0.8 copy-done
  32.4 1.8 shard_map.67
  34.2 2.2 %shard_map.68 = (f32[8,8,128]{2,1,0:T(8,128)S(1)}, bf16[3072,128]{1,0:T(8,128)(2,1)S(1)}, f32[24,128]{1,0:T(8,128)S(1)}) custom-call(s32[1]{0:T(128)} %bitcast.1.core_ref, bf16[1536,128]{1,0:T(8,128)(2,1)S(1)} %bitcast.19, bf16[1536,128]{1,0:T(8,128)(2,1)S(1)} %bitcast.30, bf16[1024,128]{1,0:T(8,128)(2,1)S(1)} %bitcast.10, f32[24,128]{1,0:T(8,128)S(1)} %bitcast.21, ...), custom_call_target="tpu_custom_call" | custom-call | flops 402653184 | bytes 1896452 | tf_op jit(solution)/shard_map/pallas_call | solution.py:315
  36.4 8.6 %all_to_all.52.from_ref = f32[8,8,128]{2,1,0:T(8,128)S(1)} all-to-all(f32[8,8,128]{2,1,0:T(8,128)S(1)} %get-tuple-element.24), channel_id=1, replica_groups=mesh['row'=8,'col'=16] {'row'}, dimensions={0} | all-to-all | bytes 65536 | tf_op jit(solution)/shard_map/all_to_all | solution.py:345
  45.0 17.4 %shard_map.69 = (f32[16,24,128]{2,1,0:T(8,128)S(1)}, f32[8,128]{1,0:T(8,128)S(1)}, f32[24,128]{1,0:T(8,128)S(1)}, bf16[1024,3072]{1,0:T(8,128)(2,1)S(1)}) custom-call(bf16[1024,128]{1,0:T(8,128)(2,1)S(1)} %bitcast.11, bf16[3072,128]{1,0:T(8,128)(2,1)S(1)} %get-tuple-element.23.right_ref.gen_ref, f32[8,128]{1,0:T(8,128)S(1)} %bitcast.26, ...), custom_call_target="tpu_custom_call" | custom-call | flops 805306368 | bytes 7589888 | tf_op jit(solution)/shard_map/pallas_call | solution.py:315
  62.5 11.7 %all_to_all.53.from_ref = f32[16,24,128]{2,1,0:T(8,128)S(1)} all-to-all(f32[16,24,128]{2,1,0:T(8,128)S(1)} %get-tuple-element.26.first_ref), channel_id=1, replica_groups=mesh['row'=8,'col'=16] {'col'}, dimensions={0} | all-to-all | bytes 393216 | tf_op jit(solution)/shard_map/all_to_all | solution.py:348
  74.2 14.5 %shard_map.70 = f32[8,8,128]{2,1,0:T(8,128)S(1)} custom-call(bf16[1024,3072]{1,0:T(8,128)(2,1)S(1)} %get-tuple-element.25.matrix_ref, bf16[1024,128]{1,0:T(8,128)(2,1)S(1)} %bitcast.12, bf16[3072,128]{1,0:T(8,128)(2,1)S(1)} %get-tuple-element.23.right_ref.gen_ref, f32[24,128]{1,0:T(8,128)S(1)} %bitcast.22, f32[16,24,128]{2,1,0:T(8,128)S(1)} %all_to_all.53.from_ref, ...), custom_call_target="tpu_custom_call" | custom-call | flops 805306368 | bytes 7794688 | tf_op jit(solution)/shard_map/pallas_call | solution.py:315
  88.7 8.6 %all_to_all.54.from_ref = f32[8,8,128]{2,1,0:T(8,128)S(1)} all-to-all(f32[8,8,128]{2,1,0:T(8,128)S(1)} %shard_map.70), channel_id=1, replica_groups=mesh['row'=8,'col'=16] {'row'}, dimensions={0} | all-to-all | bytes 65536 | tf_op jit(solution)/shard_map/all_to_all | solution.py:345
  97.3 1.1 shard_map.71
  98.4 11.5 %all_to_all.55.from_ref = f32[16,24,128]{2,1,0:T(8,128)S(1)} all-to-all(f32[16,24,128]{2,1,0:T(8,128)S(1)} %shard_map.71), channel_id=1, replica_groups=mesh['row'=8,'col'=16] {'col'}, dimensions={0} | all-to-all | bytes 393216 | tf_op jit(solution)/shard_map/all_to_all | solution.py:348
  109.9 1.5 shard_map.72
  111.4 8.6 %all_to_all.56.from_ref = f32[8,8,128]{2,1,0:T(8,128)S(1)} all-to-all(f32[8,8,128]{2,1,0:T(8,128)S(1)} %shard_map.72), channel_id=1, replica_groups=mesh['row'=8,'col'=16] {'row'}, dimensions={0} | all-to-all | bytes 65536 | tf_op jit(solution)/shard_map/all_to_all | solution.py:345
  120.0 1.1 shard_map.73
  121.1 24.2 %all_to_all.57.from_ref = f32[16,24,128]{2,1,0:T(8,128)S(1)} all-to-all(f32[16,24,128]{2,1,0:T(8,128)S(1)} %shard_map.73), channel_id=1, replica_groups=mesh['row'=8,'col'=16] {'col'}, dimensions={0} | all-to-all | bytes 393216 | tf_op jit(solution)/shard_map/all_to_all | solution.py:348
  145.4 1.5 shard_map.74
  146.9 20.9 %all_to_all.58.from_ref = f32[8,8,128]{2,1,0:T(8,128)S(1)} all-to-all(f32[8,8,128]{2,1,0:T(8,128)S(1)} %shard_map.74), channel_id=1, replica_groups=mesh['row'=8,'col'=16] {'row'}, dimensions={0} | all-to-all | bytes 65536 | tf_op jit(solution)/shard_map/all_to_all | solution.py:345
  167.8 2.7 %shard_map.75 = (f32[8,128]{1,0:T(8,128)}, f32[24,128]{1,0:T(8,128)S(1)}, f32[8,192,128]{2,1,0:T(8,128)S(1)}, f32[8,192,128]{2,1,0:T(8,128)S(1)}) custom-call(s32[1]{0:T(128)} %bitcast.1.core_ref, bf16[1024,3072]{1,0:T(8,128)(2,1)S(1)} %get-tuple-element.25.matrix_ref, bf16[1024,128]{1,0:T(8,128)(2,1)S(1)} %bitcast.17, ...), custom_call_target="tpu_custom_call" | custom-call | flops 805306368 | bytes 8986628 | tf_op jit(solution)/shard_map/pallas_call | solution.py:315
  170.5 0.1 convert_element_type.12
  170.6 0.1 collective-permute-start.1
  170.7 0.5 collective-permute-start.2
  171.2 1.2 collective-permute-done.1
  172.4 0.1 convert_element_type.13.came_ref
  172.5 0.7 shard_map.76
  173.2 0.1 convert_element_type.14
  173.2 14.2 %all_to_all.59 = f16[8,240,128]{2,1,0:T(8,128)(2,1)S(1)} all-to-all(f16[8,240,128]{2,1,0:T(8,128)(2,1)S(1)} %convert_element_type.14), channel_id=1, replica_groups={{0,2,4,6,8,10,12,14},{1,3,5,7,9,11,13,15},{16,18,20,22,24,26,28,30},{17..., dimensions={0} | all-to-all | bytes 983040 | tf_op jit(solution)/shard_map/all_to_all | solution.py:351
  187.5 0.1 convert_element_type.15.all_ref
  187.5 1.1 shard_map.77
  (9 shorter events, 0.0 us)
Async XLA Ops:
  0.6 44.4 %copy-start.3 = (f32[1024]{0:T(1024)S(1)}, f32[1024]{0:T(1024)}, u32[]{:S(2)}) copy-start(f32[1024]{0:T(1024)} %param.7) | copy-start | bytes 12292
  31.6 42.5 %copy-start.1 = (f32[3072]{0:T(1024)S(1)}, f32[3072]{0:T(1024)}, u32[]{:S(2)}) copy-start(f32[3072]{0:T(1024)} %param.6) | copy-start | bytes 36868
  31.6 2.6 %collective-permute-start = (bf16[8,192,128]{2,1,0:T(8,128)(2,1)S(1)}, bf16[8,192,128]{2,1,0:T(8,128)(2,1)S(1)}, u32[]{:S(2)}, u32[]{:S(2)}) collective-permute-start(bf16[8,192,128]{2,1,0:T(8,128)(2,1)S(1)} %all_to_all.51), channel_id=1, source_target_pairs={{0,1},{1,0},{2,3},{3,2},{4,5},{5,4},{6,7},{7,6},{8,9},{9,8},{10,11... | collective-permute-start | bytes 1179656 | tf_op jit(solution)/shard_map/ppermute | solution.py:359
  31.6 0.8 copy-start
  167.8 19.7 %copy-start.2 = (bf16[192,128]{1,0:T(8,128)(2,1)S(1)}, bf16[192,128]{1,0:T(8,128)(2,1)}, u32[]{:S(2)}) copy-start(bf16[192,128]{1,0:T(8,128)(2,1)} %points_ref.1) | copy-start | bytes 147460
  170.6 1.8 collective-permute-start.1
  170.7 1.8 collective-permute-start.2

commit v2 on v1

--- a/solution.py
+++ b/solution.py
@@ -162,6 +162,12 @@
     return jnp.where(core == 0, chosen[0], chosen[1])
 
 
+def fan_kernel(obs_ref, gen_ref, mass_ref, obs_out_ref, gen_out_ref, mass_out_ref):
+    spread(obs_out_ref, obs_ref[...])
+    spread(gen_out_ref, gen_ref[...])
+    mass_out_ref[...] = mass_ref[...]
+
+
 def half_kernel(count, core_ref, same_ref, right_ref, mass_ref, out_ref, right_sq_ref, wide_ref, shift_ref, total_ref):
     right_sq_ref[...] = squares(right_ref[...])
     mass = of_core(mass_ref[...], core_ref[0], count)
@@ -171,7 +177,7 @@
 
 def first_kernel(
     count, core_ref, same_ref, other_ref, right_ref, mass_ref, half_ref,
-    out_ref, left_ref, sq_ref, wide_ref, shift_ref, total_ref,
+    out_ref, left_ref, wide_ref, shift_ref, total_ref,
 ):
     core = core_ref[0]
     own = same_ref.shape[0] // count
@@ -179,7 +185,6 @@
         rows = pl.ds(k * own, own)
         left_ref[pl.ds(pl.multiple_of((2 * k + core) * own, 64), own), :] = same_ref[rows, :]
         left_ref[pl.ds(pl.multiple_of((2 * k + 1 - core) * own, 64), own), :] = other_ref[rows, :]
-    sq_ref[...] = squares(left_ref[...])
     mass = of_core(mass_ref[...], 1 - core, count)
     widen(mass - 0.5 * squares(other_ref[...]), wide_ref)
     result = sampled_pass(other_ref, right_ref, wide_ref, shift_ref, total_ref)
@@ -246,9 +251,19 @@
     return (gain > STEEP) | (gain < -FAINT)
 
 
+def squares_kernel(points_ref, out_ref):
+    out_ref[...] = squares(points_ref[...])
+
+
+def in_halves(values):
+    spaced = values * 8193.0
+    high = spaced - (spaced - values)
+    return high, values - high
+
+
 def mean_kernel(
     core_ref, matrix_ref, left_ref, right_ref, mass_ref, from_ref, left_add_ref, right_add_ref, left_sq_ref,
-    potential_ref, out_ref, keep_ref, send_ref, wide_ref, shift_ref, total_ref, mean_ref,
+    potential_ref, keep_ref, send_ref, wide_ref, shift_ref, total_ref, mean_ref,
 ):
     offset = 2.0 * mass_ref[...] - lse_over(planes(from_ref))
     potential_ref[...] = 2.0 * (offset - mass_ref[...]) + left_sq_ref[...]
@@ -265,26 +280,30 @@
         store_row(total_ref, chunk * CHUNK // LANES, total)
         mean_ref[across, :] = jnp.transpose((sums[:LANES, :] + sums[LANES : 2 * LANES, :]) / total)
     close_pass(left_ref, right_ref, offset, wild(gain), right_add_ref, wide_ref, shift_ref, total_ref, mean_ref)
-    out_ref[...] = shift_ref[...] + jnp.log(total_ref[...])
     core = core_ref[0]
     count, own, _ = keep_ref.shape
     for k in range(count):
         keep_ref[k] = mean_ref[pl.ds(pl.multiple_of((2 * k + core) * own, 64), own), :]
-        send_ref[k] = mean_ref[pl.ds(pl.multiple_of((2 * k + 1 - core) * own, 64), own), :]
-
-
-def pair_kernel(core_ref, keep_ref, came_ref, lse_ref, came_lse_ref, out_ref, wide_ref):
+        send_ref[k * own : (k + 1) * own, :] = mean_ref[pl.ds(pl.multiple_of((2 * k + 1 - core) * own, 64), own), :]
+    lines = total_ref.shape[0]
+    high, low = in_halves(shift_ref[...] + jnp.log(total_ref[...]))
+    send_ref[count * own : count * own + lines, :] = high
+    send_ref[count * own + lines :, :] = low
+
+
+def pair_kernel(core_ref, keep_ref, came_ref, lse_ref, out_ref, wide_ref):
     core = core_ref[0]
     count, own, _ = keep_ref.shape
-    both = lse_over([lse_ref[...], came_lse_ref[...]])
-    lines = both.shape[0]
-    spaced = both * 8193.0
-    high = spaced - (spaced - both)
-    low = both - high
-    widen(jnp.exp(lse_ref[...] - both), wide_ref)
+    lines = lse_ref.shape[0] // 2
+    mine = lse_ref[:lines, :] + lse_ref[lines:, :]
+    after = count * own
+    both = lse_over([mine, came_ref[after : after + lines, :] + came_ref[after + lines :, :]])
+    high, low = in_halves(both)
+    widen(jnp.exp(mine - both), wide_ref)
     for k in range(count):
         share = wide_ref[pl.ds(pl.multiple_of((2 * k + core) * own, 64), own), :]
-        out_ref[k, :own, :] = came_ref[k] + share * (keep_ref[k] - came_ref[k])
+        came = came_ref[k * own : (k + 1) * own, :]
+        out_ref[k, :own, :] = came + share * (keep_ref[k] - came)
         out_ref[k, own : own + lines, :] = high
         out_ref[k, own + lines :, :] = low
 
@@ -352,8 +371,19 @@
 
     mass_gen = log_mass_gen.reshape(lines, LANES)
     mass_obs = log_mass_obs.reshape(obs_lines, LANES)
-    obs = over_row(jnp.broadcast_to(points_obs[None], (n_row,) + points_obs.shape)).reshape(m, LANES)
-    gen_copies = jnp.broadcast_to(points_gen[None], (half,) + points_gen.shape)
+    obs_copies, gen_copies, mass_gen = pl.pallas_call(
+        fan_kernel,
+        grid=(1,),
+        out_shape=[
+            jax.ShapeDtypeStruct((n_row,) + points_obs.shape, points_obs.dtype),
+            jax.ShapeDtypeStruct((half,) + points_gen.shape, points_gen.dtype),
+            f32(lines, LANES),
+        ],
+        in_specs=[pl.BlockSpec(x.shape, lambda step: (0, 0)) for x in (points_obs, points_gen, mass_gen)],
+        out_specs=[VMEM] * 3,
+        compiler_params=pltpu.CompilerParams(vmem_limit_bytes=28 * 2**20),
+    )(points_obs, points_gen, mass_gen)
+    obs = over_row(obs_copies).reshape(m, LANES)
     obs, gen_copies = lax.optimization_barrier((obs, gen_copies))
     same = over_chips(gen_copies)
     other = lax.ppermute(same, "col", pair)
@@ -371,10 +401,10 @@
         [wide_scratch(n // 2), small, small],
         **half_cost,
     )
-    col_own, gen, gen_sq = call(
+    col_own, gen = call(
         functools.partial(first_kernel, half),
         (core, same, other, obs, mass_gen, half_own),
-        [col_out, jax.ShapeDtypeStruct((n, LANES), points_gen.dtype), f32(lines, LANES)],
+        [col_out, jax.ShapeDtypeStruct((n, LANES), points_gen.dtype)],
         [wide_scratch(n // 2), small, small],
         **half_cost,
     )
@@ -407,17 +437,21 @@
             **product_cost,
         )
         row_all = over_col(row_own)
-    potential_obs, row_lse, keep, send = call(
+    potential_obs, keep, send = call(
         mean_kernel,
         (core, matrix, obs, gen, mass_obs, col_all, obs_add, gen_add, obs_sq),
-        [f32(obs_lines, LANES), f32(lines, LANES), f32(half, own, LANES), f32(half, own, LANES)],
+        [f32(obs_lines, LANES), f32(half, own, LANES), f32(n // 2 + 2 * lines, LANES)],
         [wide_scratch(m), gen_small, gen_small, wide_scratch(n)],
         **product_cost,
     )
-    came = lax.ppermute(send.astype(jnp.float16), "col", pair).astype(jnp.float32)
-    came_lse = lax.ppermute(row_lse, "col", pair)
+    send = send.astype(jnp.float16)
+    came = lax.ppermute(send, "col", pair).astype(jnp.float32)
+    mine = send[n // 2 :, :].astype(jnp.float32)
+    gen_last, _ = lax.optimization_barrier((gen, send))
+    (gen_sq,) = call(squares_kernel, (gen_last,), [f32(lines, LANES)], [])
+    came, gen_sq = lax.optimization_barrier((came, gen_sq))
     (joined,) = call(
-        pair_kernel, (core, keep, came, row_lse, came_lse), [f32(half, own + 2 * lines, LANES)], [wide_scratch(n)]
+        pair_kernel, (core, keep, came, mine), [f32(half, own + 2 * lines, LANES)], [wide_scratch(n)]
     )
     joined_all = over_chips(joined.astype(jnp.float16)).astype(jnp.float32)
     span = own // LANES + 1

time: 189 us -> 191 us (1.011)
  Pallas kernels: 45.6 us -> 71.7 us
  blocking collectives: 138 us -> 115 us
    pallas_call x11 -> x12, Pallas kernels: 45.6 us -> 71.6 us  [call(): pl.pallas_call(kernel, out_shape=outs, in_specs=[SMEM if x.dtype == jnp.i...]
    all_to_all x5, blocking collectives: 60.2 us -> 48 us  [over_row(): return lax.all_to_all(blocks, 'row', 0, 0)]
    all_to_all x3, blocking collectives: 47.4 us -> 37.2 us  [over_col(): return lax.all_to_all(blocks, 'col', 0, 0)]
  transfers between devices with their start and end apart: 3 -> 2, of which waited for: 1 -> 1; matrix products, arithmetic and copies ran while one was open for 0% -> 0% of each run, Pallas kernels for 1% -> 1%
where the time goes in v2:
time: 191 us
  blocking collectives  115 us (60%)
  Pallas kernels  71.7 us (38%)
  local copies, waits for them, and re-layouts  2.26 us (1%)
    pallas_call x12, Pallas kernels, call(): pl.pallas_call(kernel, out_shape=outs, in_specs=[SMEM if x.dtype == jnp.i...  71.6 us
    all_to_all x5, blocking collectives, over_row(): return lax.all_to_all(blocks, 'row', 0, 0)  48 us
    all_to_all x3, blocking collectives, over_col(): return lax.all_to_all(blocks, 'col', 0, 0)  37.2 us
    all_to_all x2, blocking collectives, over_chips(): return lax.all_to_all(blocks, 'col', 0, 0, axis_index_groups=groups)  30.1 us
  transfers between devices with their start and end apart: 2, of which 1 were waited for; matrix products, arithmetic and copies ran while one was open for 0% of the time, Pallas kernels for 1%

profile of v2, /device:TPU:0, one launch (start us, length us, event | category | flops | bytes accessed | tf_op | source)
XLA Modules:
  0.0 191.5 jit_solution(9468083607865596442)
XLA Ops:
  0.6 0.8 copy-done
  1.4 0.8 copy-done.3
  2.2 0.7 copy-done.4
  2.9 0.1 shard_map.67
  3.0 13.4 %all_to_all.50 = bf16[8,128,128]{2,1,0:T(8,128)(2,1)S(1)} all-to-all(bf16[8,128,128]{2,1,0:T(8,128)(2,1)S(1)} %get-tuple-element.24), channel_id=1, replica_groups=mesh['row'=8,'col'=16] {'row'}, dimensions={0} | all-to-all | bytes 524288 | tf_op jit(solution)/shard_map/all_to_all | solution.py:364
  16.4 15.9 %all_to_all.51 = bf16[8,192,128]{2,1,0:T(8,128)(2,1)S(1)} all-to-all(bf16[8,192,128]{2,1,0:T(8,128)(2,1)S(1)} %get-tuple-element.27), channel_id=1, replica_groups={{0,2,4,6,8,10,12,14},{1,3,5,7,9,11,13,15},{16,18,20,22,24,26,28,30},{17..., dimensions={0} | all-to-all | bytes 786432 | tf_op jit(solution)/shard_map/all_to_all | solution.py:370
  32.3 1.8 shard_map.68
  34.1 1.7 shard_map.69
  35.8 8.6 %all_to_all.52.from_ref = f32[8,8,128]{2,1,0:T(8,128)S(1)} all-to-all(f32[8,8,128]{2,1,0:T(8,128)S(1)} %get-tuple-element.31), channel_id=1, replica_groups=mesh['row'=8,'col'=16] {'row'}, dimensions={0} | all-to-all | bytes 65536 | tf_op jit(solution)/shard_map/all_to_all | solution.py:364
  44.5 17.5 %shard_map.70 = (f32[16,24,128]{2,1,0:T(8,128)S(1)}, f32[8,128]{1,0:T(8,128)S(1)}, f32[24,128]{1,0:T(8,128)S(1)}, bf16[1024,3072]{1,0:T(8,128)(2,1)S(1)}) custom-call(bf16[1024,128]{1,0:T(8,128)(2,1)S(1)} %bitcast.11, bf16[3072,128]{1,0:T(8,128)(2,1)S(1)} %get-tuple-element.39.right_ref.gen_ref.points_ref, f32[8,128]{1,0:T(8,128)S(1)} %bitcast.20, ...), custom_call_target="tpu_custom_call" | custom-call | flops 805306368 | bytes 7589888 | tf_op jit(solution)/shard_map/pallas_call | solution.py:334
  62.0 14.2 %all_to_all.53.from_ref = f32[16,24,128]{2,1,0:T(8,128)S(1)} all-to-all(f32[16,24,128]{2,1,0:T(8,128)S(1)} %get-tuple-element.33.first_ref), channel_id=1, replica_groups=mesh['row'=8,'col'=16] {'col'}, dimensions={0} | all-to-all | bytes 393216 | tf_op jit(solution)/shard_map/all_to_all | solution.py:367
  76.1 14.5 %shard_map.71 = f32[8,8,128]{2,1,0:T(8,128)S(1)} custom-call(bf16[1024,3072]{1,0:T(8,128)(2,1)S(1)} %get-tuple-element.32.matrix_ref, bf16[1024,128]{1,0:T(8,128)(2,1)S(1)} %bitcast.12, bf16[3072,128]{1,0:T(8,128)(2,1)S(1)} %get-tuple-element.39.right_ref.gen_ref.points_ref, f32[24,128]{1,0:T(8,128)S(1)} %get-tuple-element.28.mass_ref, ...), custom_call_target="tpu_custom_call" | custom-call | flops 805306368 | bytes 7794688 | tf_op jit(solution)/shard_map/pallas_call | solution.py:334
  90.7 8.7 %all_to_all.54.from_ref = f32[8,8,128]{2,1,0:T(8,128)S(1)} all-to-all(f32[8,8,128]{2,1,0:T(8,128)S(1)} %shard_map.71), channel_id=1, replica_groups=mesh['row'=8,'col'=16] {'row'}, dimensions={0} | all-to-all | bytes 65536 | tf_op jit(solution)/shard_map/all_to_all | solution.py:364
  99.4 1.1 shard_map.72
  100.5 11.6 %all_to_all.55.from_ref = f32[16,24,128]{2,1,0:T(8,128)S(1)} all-to-all(f32[16,24,128]{2,1,0:T(8,128)S(1)} %shard_map.72), channel_id=1, replica_groups=mesh['row'=8,'col'=16] {'col'}, dimensions={0} | all-to-all | bytes 393216 | tf_op jit(solution)/shard_map/all_to_all | solution.py:367
  112.1 14.4 %shard_map.73 = f32[8,8,128]{2,1,0:T(8,128)S(1)} custom-call(bf16[1024,3072]{1,0:T(8,128)(2,1)S(1)} %get-tuple-element.32.matrix_ref, bf16[1024,128]{1,0:T(8,128)(2,1)S(1)} %bitcast.14, bf16[3072,128]{1,0:T(8,128)(2,1)S(1)} %get-tuple-element.39.right_ref.gen_ref.points_ref, f32[24,128]{1,0:T(8,128)S(1)} %get-tuple-element.28.mass_ref, ...), custom_call_target="tpu_custom_call" | custom-call | flops 805306368 | bytes 7794688 | tf_op jit(solution)/shard_map/pallas_call | solution.py:334
  126.5 8.6 %all_to_all.56.from_ref = f32[8,8,128]{2,1,0:T(8,128)S(1)} all-to-all(f32[8,8,128]{2,1,0:T(8,128)S(1)} %shard_map.73), channel_id=1, replica_groups=mesh['row'=8,'col'=16] {'row'}, dimensions={0} | all-to-all | bytes 65536 | tf_op jit(solution)/shard_map/all_to_all | solution.py:364
  135.1 1.1 shard_map.74
  136.2 11.5 %all_to_all.57.from_ref = f32[16,24,128]{2,1,0:T(8,128)S(1)} all-to-all(f32[16,24,128]{2,1,0:T(8,128)S(1)} %shard_map.74), channel_id=1, replica_groups=mesh['row'=8,'col'=16] {'col'}, dimensions={0} | all-to-all | bytes 393216 | tf_op jit(solution)/shard_map/all_to_all | solution.py:367
  147.7 14.4 %shard_map.75 = f32[8,8,128]{2,1,0:T(8,128)S(1)} custom-call(bf16[1024,3072]{1,0:T(8,128)(2,1)S(1)} %get-tuple-element.32.matrix_ref, bf16[1024,128]{1,0:T(8,128)(2,1)S(1)} %bitcast.16, bf16[3072,128]{1,0:T(8,128)(2,1)S(1)} %get-tuple-element.39.right_ref.gen_ref.points_ref, f32[24,128]{1,0:T(8,128)S(1)} %get-tuple-element.28.mass_ref, ...), custom_call_target="tpu_custom_call" | custom-call | flops 805306368 | bytes 7794688 | tf_op jit(solution)/shard_map/pallas_call | solution.py:334
  162.0 8.6 %all_to_all.58.from_ref = f32[8,8,128]{2,1,0:T(8,128)S(1)} all-to-all(f32[8,8,128]{2,1,0:T(8,128)S(1)} %shard_map.75), channel_id=1, replica_groups=mesh['row'=8,'col'=16] {'row'}, dimensions={0} | all-to-all | bytes 65536 | tf_op jit(solution)/shard_map/all_to_all | solution.py:364
  170.7 2.7 %shard_map.76 = (f32[8,128]{1,0:T(8,128)}, f32[8,192,128]{2,1,0:T(8,128)S(1)}, f32[1584,128]{1,0:T(8,128)S(1)}) custom-call(s32[1]{0:T(128)} %bitcast.1.core_ref, bf16[1024,3072]{1,0:T(8,128)(2,1)S(1)} %get-tuple-element.32.matrix_ref, bf16[1024,128]{1,0:T(8,128)(2,1)S(1)} %bitcast.17, bf16[3072,128]{1,0:T(8,128)(2,1)S(1)} %get-tuple-element.39.right_ref.gen_ref.points_ref, ...), custom_call_target="tpu_custom_call" | custom-call | flops 805306368 | bytes 8998916 | tf_op jit(solution)/shard_map/pallas_call | solution.py:334
  173.4 0.1 convert_element_type.15
  173.5 0.1 collective-permute-start.1
  173.6 0.6 shard_map.77.sq_ref
  174.1 1.2 collective-permute-done.1
  175.3 0.1 convert_element_type.16.came_ref
  175.3 0.7 shard_map.78
  176.1 0.1 convert_element_type.18
  176.1 14.2 %all_to_all.59 = f16[8,240,128]{2,1,0:T(8,128)(2,1)S(1)} all-to-all(f16[8,240,128]{2,1,0:T(8,128)(2,1)S(1)} %convert_element_type.18), channel_id=1, replica_groups={{0,2,4,6,8,10,12,14},{1,3,5,7,9,11,13,15},{16,18,20,22,24,26,28,30},{17..., dimensions={0} | all-to-all | bytes 983040 | tf_op jit(solution)/shard_map/all_to_all | solution.py:370
  190.3 0.1 convert_element_type.19.all_ref
  190.4 1.1 shard_map.79
  (10 shorter events, 0.0 us)
Async XLA Ops:
  0.6 0.8 copy-start
  1.4 0.8 copy-start.3
  2.2 0.7 copy-start.4
  2.9 41.6 %copy-start.2 = (f32[1024]{0:T(1024)S(1)}, f32[1024]{0:T(1024)}, u32[]{:S(2)}) copy-start(f32[1024]{0:T(1024)} %param.7) | copy-start | bytes 12292
  32.3 1.8 collective-permute-start
  173.4 17.0 %copy-start.1 = (bf16[192,128]{1,0:T(8,128)(2,1)S(1)}, bf16[192,128]{1,0:T(8,128)(2,1)}, u32[]{:S(2)}) copy-start(bf16[192,128]{1,0:T(8,128)(2,1)} %points_ref.1) | copy-start | bytes 147460
  173.5 1.8 collective-permute-start.1
